TPU v7x, 256 devices: a whole 4x4x8 slice. The times are simulated.
256 devices in a mesh: dp: 2 (over core), row: 16 (over y, x), col: 8 (over z).
Axes of the slice: x: 4, y: 4, z: 8, core: 2. Of those that a mesh axis runs over, the one named last changes fastest.
Arguments:
- activations: bfloat16 [2048, 8192], P('dp', 'col'), may hold values from -6 to 6
- grad_outputs: bfloat16 [2048, 8192], P('dp', 'row'), may hold values from -6 to 6
- act_basis: bfloat16 [8192, 8192], P('col', 'row'), may hold values from -0.0625 to 0.0625
- grad_basis: bfloat16 [8192, 8192], P('row', 'col'), may hold values from -0.0625 to 0.0625
- seq_lengths: int32 [2, 4], P('dp'), may hold values from 1 to 512, 1024 in all within a row
- old_eigen: float32 [8192, 8192], P('row', ('col', 'dp')), may hold values from 0.01 to 1
Outputs:
- new_eigen: float32 [8192, 8192], P('row', ('col', 'dp'))
Inputs may be any that keep to these rules, and one draw needn't show every extreme that they name: `seq_lengths`: each row sums to 1024, and its largest entry is exactly 512.
All inputs are finite; a program needn't handle non-finite values.
Results may differ from a plain program's by a relative error of at most 0.0015.
Values may be sent and summed in bfloat16 or wider, within the bound.
A program may use at most 64 MiB of HBM per device.

v0:
```python
import jax
import jax.numpy as jnp
from jax import lax
from jax.sharding import PartitionSpec as P


def local(activations, grad_outputs, act_basis, grad_basis, seq_lengths, old_eigen):
    tokens = activations.shape[0]
    act_rot = lax.psum(
        jnp.dot(activations, act_basis, preferred_element_type=jnp.float32), "col"
    ).astype(jnp.bfloat16)
    grad_rot = lax.psum(
        jnp.dot(grad_outputs, grad_basis, preferred_element_type=jnp.float32), "row"
    ).astype(jnp.bfloat16)
    lengths = seq_lengths[0]
    starts = jnp.cumsum(lengths) - lengths
    position = jnp.arange(tokens, dtype=jnp.int32)
    squares = jnp.zeros((act_rot.shape[1], grad_rot.shape[1]), jnp.float32)
    for member in range(lengths.shape[0]):
        seq_start = starts[member]
        seq_end = seq_start + lengths[member]
        inside = (position >= seq_start) & (position < seq_end)
        act_block = jnp.where(inside[:, None], act_rot, jnp.zeros((), jnp.bfloat16))
        coefficient = lax.dot_general(
            act_block, grad_rot, (((0,), (0,)), ((), ())), preferred_element_type=jnp.float32
        )
        squares = squares + coefficient * coefficient
    fresh_term = lax.psum_scatter(squares, "dp", scatter_dimension=1, tiled=True) / float(
        lax.axis_size("dp") * tokens
    )
    return 0.9 * old_eigen + 0.1 * fresh_term


def solution(mesh):
    return jax.shard_map(
        local,
        mesh=mesh,
        in_specs=(
            P("dp", "col"),
            P("dp", "row"),
            P("col", "row"),
            P("row", "col"),
            P("dp", None),
            P("row", ("col", "dp")),
        ),
        out_specs=P("row", ("col", "dp")),
        check_vma=False,
    )
```

profile of v0, /device:TPU:1, one launch (start us, length us, event | category | flops | bytes accessed | tf_op | source)
XLA Modules:
  0.0 229.3 jit_solution(11151382079066652406)
XLA Ops:
  6.5 0.0 copy-start
  6.5 0.0 reduce-scatter.2.cloned.1.call-start
  6.5 1.5 fusion.23
  8.1 0.8 reduce-window.9
  8.9 0.7 bitcast_subtract_fusion
  9.5 0.6 fusion.24
  11.4 0.7 fusion.18
  13.3 0.6 fusion.16
  15.0 0.6 fusion.15
  17.0 0.6 fusion.17
  17.6 0.0 copy-done
  17.6 3.8 %fusion.25 = f32[1024,512]{1,0:T(8,128)} fusion(bf16[1024,1024]{1,0:T(8,128)(2,1)S(1)} %copy-done, bf16[1024,512]{1,0:T(8,128)(2,1)} %param.8), kind=kOutput, calls=%fused_computation.36 | convolution fusion | flops 1073741824 | bytes 5242880 | tf_op jit(solution)/shard_map/dot_general | solution.py:10
  21.4 61.2 %all-reduce.2 = bf16[1024,512]{1,0:T(8,128)(2,1)S(1)} all-reduce(f32[1024,512]{1,0:T(8,128)} %fusion.25), channel_id=1, replica_groups=mesh['dp'=2,'row'=16,'col'=8] {'col'}, use_global_device_ids=true, to_apply=%region_1.0 | all-reduce | flops 524288 | bytes 3145728 | tf_op jit(solution)/shard_map/psum | solution.py:9
  82.6 4.7 %fusion.26 = f32[1024,1024]{1,0:T(8,128)} fusion(bf16[1024,512]{1,0:T(8,128)(2,1)} %param.7, bf16[512,1024]{1,0:T(8,128)(2,1)} %param.9), kind=kOutput, calls=%fused_computation.37 | convolution fusion | flops 1073741824 | bytes 6291456 | tf_op jit(solution)/shard_map/dot_general | solution.py:13
  87.3 95.9 %all-reduce.3 = bf16[1024,1024]{1,0:T(8,128)(2,1)} all-reduce(f32[1024,1024]{1,0:T(8,128)} %fusion.26), channel_id=1, replica_groups=mesh['dp'=2,'row'=16,'col'=8] {'row'}, use_global_device_ids=true, to_apply=%region_2.0 | all-reduce | flops 1048576 | bytes 6291456 | tf_op jit(solution)/shard_map/psum | solution.py:12
  183.2 3.1 %fusion.1 = f32[512,1024]{1,0:T(8,128)S(1)} fusion(bf16[1024,1024]{1,0:T(8,128)(2,1)} %all-reduce.3, bf16[1024,512]{1,0:T(8,128)(2,1)S(1)} %all-reduce.2, pred[1024]{0:T(1024)(128)(4,1)S(1)} %fusion.17), kind=kOutput, calls=%fused_computation.3 | convolution fusion | flops 1074266112 | bytes 5243904 | tf_op jit(solution)/shard_map/dot_general | solution.py:24
  186.3 0.0 copy-done.1
  186.3 1.4 fusion.3
  187.7 1.4 fusion.5
  189.1 3.0 %multiply_add_fusion = f32[512,1024]{1,0:T(8,128)} fusion(f32[512,1024]{1,0:T(8,128)S(1)} %fusion.1, f32[512,1024]{1,0:T(8,128)S(1)} %fusion.3, f32[512,1024]{1,0:T(8,128)S(1)} %fusion.5, bf16[1024,1024]{1,0:T(8,128)(2,1)S(1)} %copy-done.1, bf16[1024,512]{1,0:T(8,128)(2,1)S(1)} %all-reduce.2, pred[1024]{0:T(1024)(128)(4,1)S(1)} %fusion.18), kind=kOutput, calls=%fused_computation | convolution fusion | flops 1077936128 | bytes 11535360 | tf_op jit(solution)/shard_map/dot_general | solution.py:24
  192.1 0.0 reduce-scatter.2.cloned.1.call-update
  192.1 27.9 %reduce-scatter.2.cloned.1.call-done = f32[512,512]{1,0:T(8,128)} async-done(((f32[512,1024]{1,0:T(8,128)}), f32[512,512]{1,0:T(8,128)}) %reduce-scatter.2.cloned.1.call-update) | async-done | bytes 1048592 | tf_op jit(solution)/shard_map/reduce_scatter | solution.py:28
  220.1 0.0 copy-done.2
  220.1 2.4 %multiply_add_fusion.1 = f32[512,512]{1,0:T(8,128)} fusion(f32[512,512]{1,0:T(8,128)} %reduce-scatter.2.cloned.1.call-done, f32[512,512]{1,0:T(8,128)S(1)} %copy-done.2), kind=kLoop, calls=%fused_computation.1 | loop fusion | flops 786432 | bytes 3145728 | tf_op jit(solution)/shard_map/add | solution.py:31
  (2 shorter events, 0.0 us)
Async XLA Ops:
  6.5 11.1 %copy-start = (bf16[1024,1024]{1,0:T(8,128)(2,1)S(1)}, bf16[1024,1024]{1,0:T(8,128)(2,1)}, u32[]{:S(2)}) copy-start(bf16[1024,1024]{1,0:T(8,128)(2,1)} %param.6) | copy-start | bytes 6291460
  6.5 213.5 %reduce-scatter.2.cloned.1.call-start = ((), (), s32[]{:S(2)}) async-start(), calls=%async_computation.1 | async-start | bytes 3145728 | tf_op jit(solution)/shard_map/reduce_scatter | solution.py:28
  183.2 3.1 %copy-start.1 = (bf16[1024,1024]{1,0:T(8,128)(2,1)S(1)}, bf16[1024,1024]{1,0:T(8,128)(2,1)}, u32[]{:S(2)}) copy-start(bf16[1024,1024]{1,0:T(8,128)(2,1)} %all-reduce.3) | copy-start | bytes 6291460
  192.1 28.0 %copy-start.2 = (f32[512,512]{1,0:T(8,128)S(1)}, f32[512,512]{1,0:T(8,128)}, u32[]{:S(2)}) copy-start(f32[512,512]{1,0:T(8,128)} %param.11) | copy-start | bytes 3145732
Sparse Core Ops, SparseCore 0:
  192.2 27.7 reduce-scatter.1
where the time goes:
time: 230 us; the launch traced here: 229 us
  blocking collectives  157 us (68%)
  waiting for transfers between devices  28 us (12%)
  between operations  18.4 us (8%)
  matrix products  17.4 us (8%)
  other arithmetic  6.4 us (3%)
    psum x1, blocking collectives, local(): lax.psum(jnp.dot(grad_outputs, grad_basis, preferred_element_type=jnp.flo...  95.9 us
    psum x1, blocking collectives, local(): lax.psum(jnp.dot(activations, act_basis, preferred_element_type=jnp.float...  61.2 us
    reduce_scatter x1, waiting for transfers between devices, local(): lax.psum_scatter(squares, 'dp', scatter_dimension=1, tiled=True)  27.9 us
    dot_general x4, matrix products, local(): lax.dot_general(act_block, grad_rot, (((0,), (0,)), ((), ())), preferred_...  8.87 us
    dot_general x1, matrix products, local(): jnp.dot(grad_outputs, grad_basis, preferred_element_type=jnp.float32)  4.72 us
  transfers between devices with their start and end apart: 1, of which 1 were waited for; matrix products, arithmetic and copies ran while one was open for 0% of the time, Pallas kernels for 0%

commit v1 on v0

v1 whole, which is shorter than its diff:
```python
import functools

import jax
import jax.numpy as jnp
from jax import lax
from jax.experimental import pallas as pl
from jax.experimental.pallas import tpu as pltpu
from jax.sharding import PartitionSpec as P

MESH = pl.DeviceIdType.MESH
F32 = jnp.float32
BF16 = jnp.bfloat16
FAR_FIRST = (2, 1, 3)

SCHEDULE = (
    ("a", 0), ("g", 2), ("g", 1), ("g", 3), ("a", 1), ("g", 0), ("zb", 2, 0), ("zb", 3, 1), ("xd", 0),
    ("xd", 1), ("xd", 2), ("xd", 3), ("zb", 0, 2), ("zb", 1, 3), ("zc", 2, 0), ("zc", 3, 1), ("xf", 0),
    ("xf", 1), ("zc", 0, 2), ("xf", 2), ("zc", 1, 3), ("xf", 3), ("yf", 0), ("yf", 1), ("zf", 0), ("zf", 2),
    ("yf", 2), ("zf", 1), ("zf", 3), ("m", 0), ("yf", 3), ("gy", 0), ("gy", 1), ("az", 1, 0), ("gy", 2),
    ("az", 1, 2), ("gy", 3), ("az", 1, 1), ("az", 1, 3), ("m", 1), ("m", 2), ("gx", 0), ("az", 2, 0),
    ("az", 2, 2), ("gx", 1), ("az", 2, 1), ("az", 2, 3), ("gx", 2), ("m", 3), ("m", 4), ("t", 0), ("gx", 3),
    ("t", 1), ("az", 3, 0), ("az", 3, 2), ("az", 3, 1), ("az", 3, 3), ("m", 5), ("t", 2), ("m", 6),
    ("az", 4, 0), ("az", 4, 2), ("az", 4, 1), ("az", 4, 3), ("m", 7), ("gf", 0), ("gf", 1), ("gf", 2),
    ("gf", 3), ("t", 3),
)


def kernel(
    act_hbm, gout_hbm, abasis_hbm, gbasis_hbm, lengths_hbm,
    out_ref,
    act, gout, abasis, gbasis, lengths_ref,
    pg, pa, sx1, sx2, rx1, rx2, sums, sy, ry, grad,
    sz, rz, act_t, masked, squares, sq_send, sq_recv,
    in_sem, x1_ss, x1_rs, x2_ss, x2_rs, y_ss, y_rs, gy_ss, gy_rs, gx_ss, gx_rs, gf_ss, gf_rs,
    z_ss, z_rs, az_ss, az_rs, q_ss, q_rs,
):
    d = lax.axis_index("dp")
    row = lax.axis_index("row")
    z = lax.axis_index("col")
    y, x = row // 4, row % 4

    def at_z(k):
        return (d, row, (z + k) % 8)

    def along(ab, k):
        if ab == 0:
            return (d, y * 4 + (x + k) % 4, z)
        return (d, ((y + k) % 4) * 4 + x, z)

    def across(ab, k):
        return along(1 - ab, k)

    first = (x, y)
    second = (y, x)

    loads = [
        pltpu.make_async_copy(src, dst, in_sem.at[i])
        for i, (src, dst) in enumerate(
            ((gout_hbm, gout), (gbasis_hbm, gbasis), (act_hbm, act), (abasis_hbm, abasis),
             (lengths_hbm, lengths_ref))
        )
    ]
    for i in (3, 2, 4):
        loads[i].start()

    barrier = pltpu.get_barrier_semaphore()
    partners = [at_z(1), at_z(7), at_z(2), at_z(6), (1 - d, row, z)]
    for ab in range(2):
        for k in (1, 2, 3):
            partners.append(along(ab, k))
    for p in partners:
        pl.semaphore_signal(barrier, inc=1, device_id=p, device_id_type=MESH)

    pending = []

    def loop(n, body):
        lax.fori_loop(0, n, lambda i, c: (body(i), c)[1], 0)

    def copy(src, dst, ss, rs, dev):
        return pltpu.make_async_remote_copy(
            src_ref=src, dst_ref=dst, send_sem=ss, recv_sem=rs, device_id=dev, device_id_type=MESH
        )

    def send(src, dst, ss, rs, dev):
        c = copy(src, dst, ss, rs, dev)
        c.start()
        pending.append(c)

    def arrived(dst, rs, ss, dev):
        pltpu.make_async_remote_copy(
            src_ref=dst, dst_ref=dst, send_sem=ss, recv_sem=rs, device_id=dev, device_id_type=MESH
        ).wait_recv()

    def grad_dots(rel, use):
        ca = pl.multiple_of(((x + rel) % 4) * 128, 128)
        cb = pl.multiple_of(512 + ((y + rel) % 4) * 128, 128)

        def body(t):
            lhs = gout[pl.ds(pl.multiple_of(t * 256, 256), 256)]
            rhs = jnp.concatenate([gbasis[:, pl.ds(ca, 128)], gbasis[:, pl.ds(cb, 128)]], axis=1)
            res = jnp.dot(lhs, rhs, preferred_element_type=F32)
            for ab in range(2):
                use(t, ab, res[:, ab * 128:(ab + 1) * 128].reshape(2, 128, 128))

        loop(4, body)

    def x1_copy(ab, side, t):
        return copy(sx1.at[ab, 2 * t + side], rx1.at[ab, side, t], x1_ss.at[ab, side, t],
                    x1_rs.at[ab, side, t], along(ab, 1 if side == 0 else 3))

    def grad_far():
        loads[0].wait()
        loads[1].wait()

        def use(t, ab, block):
            sx1[ab, pl.ds(2 * t, 2)] = block.astype(BF16)
            for side in range(2):
                x1_copy(ab, side, t).start()

        grad_dots(2, use)
        pending.extend((4, lambda t, ab=ab, side=side: x1_copy(ab, side, t)) for ab in range(2) for side in range(2))

    def x2_copy(ab, side, t, h):
        return copy(sx2.at[ab, side, 2 * t + h], rx2.at[ab, side, 2 * t + h], x2_ss.at[ab, side, t, h],
                    x2_rs.at[ab, side, t, h], along(ab, 1 if side == 0 else 3))

    def grad_near(side):
        def use(t, ab, block):
            pg[1 + side, ab, pl.ds(2 * t, 2)] = block
            sx2[ab, side, 2 * t + 1 - side] = block[1 - side].astype(BF16)
            x2_copy(ab, side, t, 1 - side).start()

        grad_dots(1 if side == 0 else 3, use)
        pending.extend((4, lambda t, ab=ab: x2_copy(ab, side, t, 1 - side)) for ab in range(2))

    mid, par = z // 2, z % 2

    def act_dot(first_pair):
        if first_pair:
            blocks = ((mid + 2) % 4, (mid + 1 + 2 * par) % 4)
        else:
            blocks = (mid, (mid + 3 + 2 * par) % 4)
        starts = [pl.multiple_of(b * 128, 128) for b in blocks]

        def body(t):
            rhs = jnp.concatenate([abasis[:, pl.ds(c, 128)] for c in starts], axis=1)
            lhs = act[pl.ds(pl.multiple_of(t * 256, 256), 256)]
            res = jnp.dot(lhs, rhs, preferred_element_type=F32)
            for n, b in enumerate(blocks):
                pa[b, pl.ds(2 * t, 2)] = res[:, n * 128:(n + 1) * 128].reshape(2, 128, 128)

        loop(4, body)

    def own(k, p):
        c = (z + k) % 8
        return pa[c // 2, (c % 2) * 4 + p]

    def z_dev(side):
        return at_z(1 if side == 0 else 7)

    def z_send(side, stage, p):
        k = (4, 3, 2, 1)[stage] if side == 0 else (4, 5, 6, 7)[stage]
        value = own(k, p)
        for other in {0: (), 1: (), 2: (1, 0) if p in near[side] else (1,), 3: (2,)}[stage]:
            z_arrived(side, other, p)
            value = value + rz[side, other, p].astype(F32)
        sz[side, stage, p] = value.astype(BF16)
        send(sz.at[side, stage, p], rz.at[side, stage, p], z_ss.at[side, stage, p],
             z_rs.at[side, stage, p], z_far(side) if stage == 0 else z_dev(side))

    def z_arrived(side, stage, p):
        arrived(rz.at[side, stage, p], z_rs.at[side, stage, p], z_ss.at[side, stage, p],
                z_far(side) if stage == 0 else z_dev(side))

    def z_far(side):
        return at_z(2 if side == 0 else 6)

    near = ((0, 1), (2, 3))

    def act_first():
        loads[2].wait()
        loads[3].wait()
        loads[0].start()
        loads[1].start()
        loads[4].wait()
        act_dot(True)
        pl.semaphore_wait(barrier, len(partners))
        for stage, which in ((1, 1), (0, 0), (1, 0)):
            for i in range(2):
                z_send(0, stage, near[which][i])
                z_send(1, stage, near[1 - which][i])

    def grad_last():
        def use(t, ab, block):
            pg[0, ab, pl.ds(2 * t, 2)] = block

        grad_dots(0, use)

    def x_dep(t):
        for ab in range(2):
            for side in range(2):
                b = 2 * t + side
                arrived(rx1.at[ab, side, t], x1_rs.at[ab, side, t], x1_ss.at[ab, side, t],
                        along(ab, 1 if side == 0 else 3))
                sx2[ab, side, b] = (pg[1 + side, ab, b] + rx1[ab, side, t].astype(F32)).astype(BF16)
                c = x2_copy(ab, side, t, side)
                c.start()
                pending.append(c)

    def x_fin(t):
        for ab in range(2):
            for side in range(2):
                for h in range(2):
                    arrived(rx2.at[ab, side, 2 * t + h], x2_rs.at[ab, side, t, h], x2_ss.at[ab, side, t, h],
                            along(ab, 1 if side == 0 else 3))
            s = slice(2 * t, 2 * t + 2)
            total = pg[0, ab, s] + (rx2[ab, 0, s].astype(F32) + rx2[ab, 1, s].astype(F32))
            total = total.reshape(4, 64, 128)
            sums[ab, t] = total
            sy[ab, t] = total.astype(BF16)
            for k in FAR_FIRST:
                send(sy.at[ab, t, (second[ab] + k) % 4], ry.at[ab, t, k], y_ss.at[ab, t, k], y_rs.at[ab, t, k],
                     across(ab, k))

    def z_pair(stage):
        def run(p0, p1):
            z_send(0, stage, p0)
            z_send(1, stage, p1)
        return run

    def az_send(side, step, p):
        far = step == 4
        back = 2 if far else step - 1
        c = (z - back) % 8 if side == 0 else (z + back) % 8
        send(act_t.at[c, p], act_t.at[c, p], az_ss.at[side, step - 1, p], az_rs.at[side, step - 1, p],
             z_far(side) if far else z_dev(side))

    def az_arrived(side, step, p):
        c = (z - step) % 8 if side == 0 else (z + step) % 8
        arrived(act_t.at[c, p], az_rs.at[side, step - 1, p], az_ss.at[side, step - 1, p],
                z_far(side) if step == 4 else z_dev(side))

    def z_fin(p):
        for side in range(2):
            z_arrived(side, 3, p)
        total = own(0, p) + (rz[0, 3, p].astype(F32) + rz[1, 3, p].astype(F32))
        act_t[z, p] = total.T.astype(BF16)
        for side in range(2):
            az_send(side, 1, p)

    def az(step, p):
        for side in range(2):
            if step < 4 or p in near[side]:
                az_arrived(side, step, p)
        for side in range(2):
            if step == 2 and p in near[side]:
                az_send(side, 4, p)
        for side in range(2):
            if step < 3:
                az_send(side, step + 1, p)

    def strip(ab, rel, t):
        return 4 * ab + (first[ab] + rel) % 4, 4 * t

    def y_fin(t):
        for ab in range(2):
            total = sums[ab, t, second[ab]]
            for k in (1, 3, 2):
                arrived(ry.at[ab, t, k], y_rs.at[ab, t, k], y_ss.at[ab, t, k], across(ab, k))
                total = total + ry[ab, t, k].astype(F32)
            b, r = strip(ab, 0, t)
            grad[b, r + second[ab]] = total.astype(BF16)
            part = grad.at[b, r + second[ab]]
            for k in FAR_FIRST:
                send(part, part, gy_ss.at[ab, t, k], gy_rs.at[ab, t, k], across(ab, k))

    def gy(t):
        for ab in range(2):
            b, r = strip(ab, 0, t)
            for k in (1, 3, 2):
                part = grad.at[b, r + (second[ab] + 4 - k) % 4]
                arrived(part, gy_rs.at[ab, t, k], gy_ss.at[ab, t, k], across(ab, k))
            part = grad.at[b, pl.ds(r, 4)]
            for side in range(2):
                send(part, part, gx_ss.at[ab, side, t], gx_rs.at[ab, side, t], along(ab, 1 if side == 0 else 3))

    def gx_forward(t):
        for ab in range(2):
            for side in range(2):
                b, r = strip(ab, 3 if side == 0 else 1, t)
                dev = along(ab, 1 if side == 0 else 3)
                arrived(grad.at[b, pl.ds(r, 4)], gx_rs.at[ab, side, t], gx_ss.at[ab, side, t], dev)
                part = grad.at[b, pl.ds(r + 2 * side, 2)]
                send(part, part, gf_ss.at[ab, side, t], gf_rs.at[ab, side, t], dev)

    def gf_arrived(t):
        for ab in range(2):
            for side in range(2):
                b, r = strip(ab, 2, t)
                arrived(grad.at[b, pl.ds(r + 2 * side, 2)], gf_rs.at[ab, side, t], gf_ss.at[ab, side, t],
                        along(ab, 1 if side == 0 else 3))

    toward = 1 - 2 * par
    chunks = [(z + toward * r + 8) % 8 for r in (0, 1, -1, -2, 2, 3, -3, 4)]
    places = [chunks[2 * m] // 2 for m in range(4)]
    bounds = [jnp.int32(0)]

    def mask(n):
        for s in range(5 - len(bounds)):
            bounds.append(bounds[-1] + lengths_ref[0, s])
        c = chunks[n]

        def body(p):
            start = (c % 2) * 512 + p * 128
            position = lax.broadcasted_iota(jnp.int32, (1, 128), 1) + start
            block = act_t[c, p]
            for s in range(4):
                inside = jnp.where((position >= bounds[s]) & (position < bounds[s + 1]), 1.0, 0.0).astype(BF16)
                held = block * inside
                for h in range(2):
                    masked[n // 2, h, s, :, pl.ds(pl.multiple_of(start, 128), 128)] = held[h * 64:(h + 1) * 64]

        loop(4, body)

    partner = (1 - d, row, z)

    def q_copy(m, k):
        return copy(sq_send.at[k, m], sq_recv.at[k, m], q_ss.at[k, m], q_rs.at[k, m], partner)

    def coefficients(m, k):
        blocks = (lax.rem(x + k, 4), 4 + lax.rem(y + k, 4))

        def half(h):
            lhs = masked[m, h].reshape(256, 1024)
            rhs = jnp.concatenate([grad[b].reshape(1024, 128) for b in blocks], axis=1)
            co = jnp.dot(lhs, rhs, preferred_element_type=F32)
            co = co * co
            total = (co[:64] + co[64:128]) + (co[128:192] + co[192:])
            a, b = total[:, :128], total[:, 128:]
            squares[k, m, h] = jnp.where(d == 0, a, b)
            sq_send[k, m, h] = jnp.where(d == 0, b, a).astype(BF16)

        loop(2, half)
        q_copy(m, k).start()

    def batch(n):
        if n == 0:
            loop(2, lambda i: coefficients(i, 0))
        elif n == 1:
            loop(4, lambda i: coefficients(i // 2, 1 + 2 * (i % 2)))
        elif n == 2:
            loop(3, lambda i: coefficients(2, i + i // 2))
        else:
            loop(7, lambda i: coefficients(jnp.minimum(i, 3), jnp.where(i < 3, 2, i - 3)))

    def finish(i):
        m, k = i // 4, i % 4
        q_copy(m, k).wait_recv()
        block = jnp.where(d == 0, (x + k) % 4, (y + k) % 4)
        place = jnp.where(m < 2, jnp.where(m == 0, places[0], places[1]), jnp.where(m == 2, places[2], places[3]))
        cols = pl.ds(pl.multiple_of(block * 128, 128), 128)
        for h in range(2):
            rows = pl.ds(pl.multiple_of(place * 128 + h * 64, 64), 64)
            out_ref[rows, cols] = squares[k, m, h] + sq_recv[k, m, h].astype(F32)

    def grads(rel):
        if rel == 2:
            grad_far()
        elif rel == 0:
            grad_last()
        else:
            grad_near(0 if rel == 1 else 1)

    def acts(n):
        if n == 0:
            act_first()
        else:
            act_dot(False)

    steps = {
        "a": acts, "g": grads, "zb": z_pair(2), "zc": z_pair(3), "xd": x_dep, "xf": x_fin, "zf": z_fin, "yf": y_fin,
        "az": az, "gy": gy, "gx": gx_forward, "gf": gf_arrived, "m": mask, "t": batch,
    }
    for name, *where in SCHEDULE:
        steps[name](*where)
    loop(16, finish)
    for c in pending:
        if isinstance(c, tuple):
            loop(c[0], lambda t, make=c[1]: make(t).wait_send())
        else:
            c.wait_send()
    loop(16, lambda i: q_copy(i // 4, i % 4).wait_send())


def local(activations, grad_outputs, act_basis, grad_basis, seq_lengths, old_eigen):
    vm = pltpu.VMEM
    dma = pltpu.SemaphoreType.DMA
    anywhere = pl.BlockSpec(memory_space=pltpu.HBM)
    squares = pl.pallas_call(
        kernel,
        out_shape=pltpu.VMEM((512, 512), F32),
        in_specs=[anywhere] * 5,
        out_specs=pl.BlockSpec(memory_space=pltpu.VMEM),
        scratch_shapes=[
            vm((1024, 1024), BF16), vm((1024, 512), BF16), vm((1024, 512), BF16), vm((512, 1024), BF16),
            pltpu.SMEM((1, 4), jnp.int32),
            vm((3, 2, 8, 128, 128), F32),
            vm((4, 8, 128, 128), F32),
            vm((2, 8, 128, 128), BF16),
            vm((2, 2, 8, 128, 128), BF16),
            vm((2, 2, 4, 128, 128), BF16),
            vm((2, 2, 8, 128, 128), BF16),
            vm((2, 4, 4, 64, 128), F32),
            vm((2, 4, 4, 64, 128), BF16),
            vm((2, 4, 4, 64, 128), BF16),
            vm((8, 16, 64, 128), BF16),
            vm((2, 4, 4, 128, 128), BF16),
            vm((2, 4, 4, 128, 128), BF16),
            vm((8, 4, 128, 128), BF16),
            vm((4, 2, 4, 64, 1024), BF16),
            vm((4, 4, 2, 64, 128), F32),
            vm((4, 4, 2, 64, 128), BF16),
            vm((4, 4, 2, 64, 128), BF16),
            dma((5,)),
            dma((2, 2, 4)), dma((2, 2, 4)),
            dma((2, 2, 4, 2)), dma((2, 2, 4, 2)),
            dma((2, 4, 4)), dma((2, 4, 4)),
            dma((2, 4, 4)), dma((2, 4, 4)),
            dma((2, 2, 4)), dma((2, 2, 4)),
            dma((2, 2, 4)), dma((2, 2, 4)),
            dma((2, 4, 4)), dma((2, 4, 4)),
            dma((2, 4, 4)), dma((2, 4, 4)),
            dma((4, 4)), dma((4, 4)),
        ],
        compiler_params=pltpu.CompilerParams(
            collective_id=0, has_side_effects=True, vmem_limit_bytes=48 << 20
        ),
        name="rotate_and_square",
    )(*(pltpu.with_memory_space_constraint(a, pltpu.HBM)
        for a in (activations, grad_outputs, act_basis, grad_basis, seq_lengths)))
    return 0.9 * old_eigen + (0.1 / 2048.0) * squares


def solution(mesh):
    return jax.shard_map(
        local,
        mesh=mesh,
        in_specs=(
            P("dp", "col"),
            P("dp", "row"),
            P("col", "row"),
            P("row", "col"),
            P("dp", None),
            P("row", ("col", "dp")),
        ),
        out_specs=P("row", ("col", "dp")),
        check_vma=False,
    )
```

time: 230 us -> 53.8 us (0.23)
  blocking collectives: 157 us -> 0 us
  Pallas kernels: 0 us -> 52.5 us
  waiting for transfers between devices: 28 us -> 0 us
  between operations: 18.4 us -> 0.02 us
  matrix products: 17.4 us -> 0 us
  other arithmetic: 6.4 us -> 1.22 us
    psum x2 -> x0, blocking collectives: 157 us -> none  [the longest x1 95.9 us: local(): lax.psum(jnp.dot(grad_outputs, grad_basis, preferred_element_type=jnp.flo...]
    pallas_call x0 -> x1, Pallas kernels: none -> 52.5 us  [local(): pl.pallas_call(kernel, out_shape=pltpu.VMEM((512, 512), F32), in_specs=[a...]
    reduce_scatter x1 -> x0, waiting for transfers between devices: 27.9 us -> none  [local(): lax.psum_scatter(squares, 'dp', scatter_dimension=1, tiled=True)]
    dot_general x6 -> x0, matrix products: 17.4 us -> none  [the longest x4 8.87 us: local(): lax.dot_general(act_block, grad_rot, (((0,), (0,)), ((), ())), preferred_...]
    and x4 -> x0, other arithmetic: 2.48 us -> none  [local(): inside = (position >= seq_start) & (position < seq_end)]
  transfers between devices with their start and end apart: 1 -> 0, of which waited for: 1 -> 0; matrix products, arithmetic and copies ran while one was open for 0% -> 0% of each run, Pallas kernels for 0% -> 0%
where the time goes in v1:
time: 53.8 us; the launch traced here: 53.7 us
  Pallas kernels  52.5 us (98%)
  other arithmetic  1.22 us (2%)
    pallas_call x1, Pallas kernels, local(): pl.pallas_call(kernel, out_shape=pltpu.VMEM((512, 512), F32), in_specs=[a...  52.5 us
    add x1, other arithmetic, local(): return 0.9 * old_eigen + 0.1 / 2048.0 * squares  1.22 us

profile of v1, /device:TPU:1, one launch (start us, length us, event | category | flops | bytes accessed | tf_op | source)
XLA Modules:
  0.0 53.7 jit_solution(10168593863284114423)
XLA Ops:
  0.0 0.0 copy-start
  0.0 52.5 %rotate_and_square.1 = f32[512,512]{1,0:T(8,128)S(1)} custom-call(bf16[1024,1024]{1,0:T(8,128)(2,1)} %act_hbm.1, bf16[1024,512]{1,0:T(8,128)(2,1)} %gout_hbm.1, bf16[1024,512]{1,0:T(8,128)(2,1)} %abasis_hbm.1, bf16[512,1024]{1,0:T(8,128)(2,1)} %gbasis_hbm.1, s32[1,4]{1,0:T(1,128)} %lengths_hbm.1), custom_call_target="tpu_custom_call" | custom-call | tf_op jit(solution)/shard_map/rotate_and_square/pallas_call | solution.py:399
  52.5 0.0 copy-done
  52.5 1.2 %multiply_add_fusion = f32[512,512]{1,0:T(8,128)} fusion(f32[512,512]{1,0:T(8,128)S(1)} %rotate_and_square.1, f32[512,512]{1,0:T(8,128)S(1)} %copy-done), kind=kLoop, calls=%fused_computation | loop fusion | flops 786432 | bytes 3145728 | tf_op jit(solution)/shard_map/add | solution.py:441
Async XLA Ops:
  0.0 52.5 %copy-start = (f32[512,512]{1,0:T(8,128)S(1)}, f32[512,512]{1,0:T(8,128)}, u32[]{:S(2)}) copy-start(f32[512,512]{1,0:T(8,128)} %param.11) | copy-start | bytes 3145732

commit v2 on v1

--- a/solution.py
+++ b/solution.py
@@ -14,14 +14,14 @@
 
 SCHEDULE = (
     ("a", 0), ("g", 2), ("g", 1), ("g", 3), ("a", 1), ("g", 0), ("zb", 2, 0), ("zb", 3, 1), ("xd", 0),
-    ("xd", 1), ("xd", 2), ("xd", 3), ("zb", 0, 2), ("zb", 1, 3), ("zc", 2, 0), ("zc", 3, 1), ("xf", 0),
-    ("xf", 1), ("zc", 0, 2), ("xf", 2), ("zc", 1, 3), ("xf", 3), ("yf", 0), ("yf", 1), ("zf", 0), ("zf", 2),
-    ("yf", 2), ("zf", 1), ("zf", 3), ("m", 0), ("yf", 3), ("gy", 0), ("gy", 1), ("az", 1, 0), ("gy", 2),
-    ("az", 1, 2), ("gy", 3), ("az", 1, 1), ("az", 1, 3), ("m", 1), ("m", 2), ("gx", 0), ("az", 2, 0),
-    ("az", 2, 2), ("gx", 1), ("az", 2, 1), ("az", 2, 3), ("gx", 2), ("m", 3), ("m", 4), ("t", 0), ("gx", 3),
-    ("t", 1), ("az", 3, 0), ("az", 3, 2), ("az", 3, 1), ("az", 3, 3), ("m", 5), ("t", 2), ("m", 6),
-    ("az", 4, 0), ("az", 4, 2), ("az", 4, 1), ("az", 4, 3), ("m", 7), ("gf", 0), ("gf", 1), ("gf", 2),
-    ("gf", 3), ("t", 3),
+    ("xd", 1), ("xd", 2), ("zb", 0, 2), ("xd", 3), ("zb", 1, 3), ("zc", 2, 0), ("zc", 3, 1), ("zc", 0, 2),
+    ("xf", 0), ("zc", 1, 3), ("xf", 1), ("xf", 2), ("xf", 3), ("zf", 0), ("zf", 2), ("zf", 1), ("yf", 0),
+    ("zf", 3), ("d", "zb", 1, 3), ("m", 0), ("yf", 1), ("yf", 2), ("yf", 3), ("az", 1, 0), ("az", 1, 2), ("gy", 0), ("az", 1, 1),
+    ("gy", 1), ("az", 1, 3), ("m", 1), ("m", 2), ("d", "xf", 3), ("gy", 2), ("az", 2, 0), ("gy", 3), ("az", 2, 2),
+    ("az", 2, 1), ("gx", 0), ("az", 2, 3), ("gx", 1), ("gx", 2), ("gx", 3), ("m", 3), ("d", "az", 1, 3), ("t", 0), ("m", 4),
+    ("az", 3, 0), ("az", 3, 2), ("az", 3, 1), ("az", 3, 3), ("m", 5), ("t", 1), ("m", 6), ("az", 4, 0),
+    ("az", 4, 2), ("az", 4, 1), ("az", 4, 3), ("m", 7), ("t", 2), ("d", "gx", 2), ("gf", 0), ("gf", 1), ("gf", 2), ("gf", 3),
+    ("t", 3),
 )
 
 
@@ -53,15 +53,23 @@
     first = (x, y)
     second = (y, x)
 
-    loads = [
-        pltpu.make_async_copy(src, dst, in_sem.at[i])
-        for i, (src, dst) in enumerate(
-            ((gout_hbm, gout), (gbasis_hbm, gbasis), (act_hbm, act), (abasis_hbm, abasis),
-             (lengths_hbm, lengths_ref))
-        )
-    ]
-    for i in (3, 2, 4):
-        loads[i].start()
+    mid, par = z // 2, z % 2
+    act_blocks = ((mid + 2) % 4, (mid + 1 + 2 * par) % 4, mid, (mid + 3 + 2 * par) % 4)
+
+    def columns(ref, b):
+        return ref.at[:, pl.ds(pl.multiple_of(b * 128, 128), 128)]
+
+    def quarter(ref, t):
+        return ref.at[t * 256:(t + 1) * 256]
+
+    pairs = [(columns(abasis_hbm, b), columns(abasis, b)) for b in act_blocks[:2]]
+    pairs += [(quarter(act_hbm, t), quarter(act, t)) for t in range(4)]
+    pairs += [(lengths_hbm, lengths_ref), (gbasis_hbm, gbasis)]
+    pairs += [(quarter(gout_hbm, t), quarter(gout, t)) for t in range(4)]
+    pairs += [(columns(abasis_hbm, b), columns(abasis, b)) for b in act_blocks[2:]]
+    loads = [pltpu.make_async_copy(src, dst, in_sem.at[i]) for i, (src, dst) in enumerate(pairs)]
+    for c in loads:
+        c.start()
 
     barrier = pltpu.get_barrier_semaphore()
     partners = [at_z(1), at_z(7), at_z(2), at_z(6), (1 - d, row, z)]
@@ -91,65 +99,52 @@
             src_ref=dst, dst_ref=dst, send_sem=ss, recv_sem=rs, device_id=dev, device_id_type=MESH
         ).wait_recv()
 
-    def grad_dots(rel, use):
+    def grad_dot(rel, rows):
         ca = pl.multiple_of(((x + rel) % 4) * 128, 128)
         cb = pl.multiple_of(512 + ((y + rel) % 4) * 128, 128)
-
-        def body(t):
-            lhs = gout[pl.ds(pl.multiple_of(t * 256, 256), 256)]
-            rhs = jnp.concatenate([gbasis[:, pl.ds(ca, 128)], gbasis[:, pl.ds(cb, 128)]], axis=1)
-            res = jnp.dot(lhs, rhs, preferred_element_type=F32)
-            for ab in range(2):
-                use(t, ab, res[:, ab * 128:(ab + 1) * 128].reshape(2, 128, 128))
-
-        loop(4, body)
+        rhs = jnp.concatenate([gbasis[:, pl.ds(ca, 128)], gbasis[:, pl.ds(cb, 128)]], axis=1)
+        res = jnp.dot(gout[rows], rhs, preferred_element_type=F32)
+        return [res[:, ab * 128:(ab + 1) * 128].reshape(-1, 128, 128) for ab in range(2)]
 
     def x1_copy(ab, side, t):
         return copy(sx1.at[ab, 2 * t + side], rx1.at[ab, side, t], x1_ss.at[ab, side, t],
                     x1_rs.at[ab, side, t], along(ab, 1 if side == 0 else 3))
 
     def grad_far():
-        loads[0].wait()
-        loads[1].wait()
-
-        def use(t, ab, block):
-            sx1[ab, pl.ds(2 * t, 2)] = block.astype(BF16)
-            for side in range(2):
-                x1_copy(ab, side, t).start()
-
-        grad_dots(2, use)
-        pending.extend((4, lambda t, ab=ab, side=side: x1_copy(ab, side, t)) for ab in range(2) for side in range(2))
+        loads[6].wait()
+        loads[7].wait()
+        for t in range(4):
+            loads[8 + t].wait()
+            for ab, block in enumerate(grad_dot(2, slice(t * 256, (t + 1) * 256))):
+                sx1[ab, 2 * t:2 * t + 2] = block.astype(BF16)
+            for ab in range(2):
+                for side in range(2):
+                    c = x1_copy(ab, side, t)
+                    c.start()
+                    pending.append(c)
 
     def x2_copy(ab, side, t, h):
         return copy(sx2.at[ab, side, 2 * t + h], rx2.at[ab, side, 2 * t + h], x2_ss.at[ab, side, t, h],
                     x2_rs.at[ab, side, t, h], along(ab, 1 if side == 0 else 3))
 
     def grad_near(side):
-        def use(t, ab, block):
-            pg[1 + side, ab, pl.ds(2 * t, 2)] = block
-            sx2[ab, side, 2 * t + 1 - side] = block[1 - side].astype(BF16)
-            x2_copy(ab, side, t, 1 - side).start()
-
-        grad_dots(1 if side == 0 else 3, use)
-        pending.extend((4, lambda t, ab=ab: x2_copy(ab, side, t, 1 - side)) for ab in range(2))
-
-    mid, par = z // 2, z % 2
+        for ab, block in enumerate(grad_dot(1 if side == 0 else 3, slice(0, 1024))):
+            pg[1 + side, ab] = block
+            sx2[ab, side] = block.astype(BF16)
+        for t in range(4):
+            for ab in range(2):
+                c = x2_copy(ab, side, t, 1 - side)
+                c.start()
+                pending.append(c)
 
     def act_dot(first_pair):
-        if first_pair:
-            blocks = ((mid + 2) % 4, (mid + 1 + 2 * par) % 4)
-        else:
-            blocks = (mid, (mid + 3 + 2 * par) % 4)
-        starts = [pl.multiple_of(b * 128, 128) for b in blocks]
-
-        def body(t):
-            rhs = jnp.concatenate([abasis[:, pl.ds(c, 128)] for c in starts], axis=1)
-            lhs = act[pl.ds(pl.multiple_of(t * 256, 256), 256)]
-            res = jnp.dot(lhs, rhs, preferred_element_type=F32)
-            for n, b in enumerate(blocks):
-                pa[b, pl.ds(2 * t, 2)] = res[:, n * 128:(n + 1) * 128].reshape(2, 128, 128)
-
-        loop(4, body)
+        for i in range(6) if first_pair else (12, 13):
+            loads[i].wait()
+        blocks = act_blocks[:2] if first_pair else act_blocks[2:]
+        rhs = jnp.concatenate([abasis[:, pl.ds(pl.multiple_of(b * 128, 128), 128)] for b in blocks], axis=1)
+        res = jnp.dot(act[...], rhs, preferred_element_type=F32)
+        for n, b in enumerate(blocks):
+            pa[b] = res[:, n * 128:(n + 1) * 128].reshape(8, 128, 128)
 
     def own(k, p):
         c = (z + k) % 8
@@ -178,11 +173,6 @@
     near = ((0, 1), (2, 3))
 
     def act_first():
-        loads[2].wait()
-        loads[3].wait()
-        loads[0].start()
-        loads[1].start()
-        loads[4].wait()
         act_dot(True)
         pl.semaphore_wait(barrier, len(partners))
         for stage, which in ((1, 1), (0, 0), (1, 0)):
@@ -191,10 +181,8 @@
                 z_send(1, stage, near[1 - which][i])
 
     def grad_last():
-        def use(t, ab, block):
-            pg[0, ab, pl.ds(2 * t, 2)] = block
-
-        grad_dots(0, use)
+        for ab, block in enumerate(grad_dot(0, slice(0, 1024))):
+            pg[0, ab] = block
 
     def x_dep(t):
         for ab in range(2):
@@ -316,9 +304,7 @@
             block = act_t[c, p]
             for s in range(4):
                 inside = jnp.where((position >= bounds[s]) & (position < bounds[s + 1]), 1.0, 0.0).astype(BF16)
-                held = block * inside
-                for h in range(2):
-                    masked[n // 2, h, s, :, pl.ds(pl.multiple_of(start, 128), 128)] = held[h * 64:(h + 1) * 64]
+                masked[n // 2, s, :, pl.ds(pl.multiple_of(start, 128), 128)] = block * inside
 
         loop(4, body)
 
@@ -328,40 +314,43 @@
         return copy(sq_send.at[k, m], sq_recv.at[k, m], q_ss.at[k, m], q_rs.at[k, m], partner)
 
     def coefficients(m, k):
-        blocks = (lax.rem(x + k, 4), 4 + lax.rem(y + k, 4))
-
-        def half(h):
-            lhs = masked[m, h].reshape(256, 1024)
-            rhs = jnp.concatenate([grad[b].reshape(1024, 128) for b in blocks], axis=1)
-            co = jnp.dot(lhs, rhs, preferred_element_type=F32)
-            co = co * co
-            total = (co[:64] + co[64:128]) + (co[128:192] + co[192:])
-            a, b = total[:, :128], total[:, 128:]
-            squares[k, m, h] = jnp.where(d == 0, a, b)
-            sq_send[k, m, h] = jnp.where(d == 0, b, a).astype(BF16)
-
-        loop(2, half)
-        q_copy(m, k).start()
+        blocks = ((x + k) % 4, 4 + (y + k) % 4)
+        lhs = masked[m].reshape(512, 1024)
+        rhs = jnp.concatenate([grad[b].reshape(1024, 128) for b in blocks], axis=1)
+        co = jnp.dot(lhs, rhs, preferred_element_type=F32)
+        co = co * co
+        total = (co[:128] + co[128:256]) + (co[256:384] + co[384:])
+        a, b = total[:, :128], total[:, 128:]
+        squares[k, m] = jnp.where(d == 0, a, b)
+        sq_send[k, m] = jnp.where(d == 0, b, a).astype(BF16)
+
+    tiles = (
+        ((0, 0), (0, 1), (0, 3), (1, 0), (1, 1), (1, 3)),
+        ((2, 0), (2, 1), (2, 3)),
+        ((3, 0), (3, 1), (3, 3)),
+        ((0, 2), (1, 2), (2, 2), (3, 2)),
+    )
 
     def batch(n):
         if n == 0:
-            loop(2, lambda i: coefficients(i, 0))
-        elif n == 1:
-            loop(4, lambda i: coefficients(i // 2, 1 + 2 * (i % 2)))
-        elif n == 2:
-            loop(3, lambda i: coefficients(2, i + i // 2))
+            loop(6, lambda i: coefficients(i // 3, i % 3 + i % 3 // 2))
+        elif n == 3:
+            loop(4, lambda i: coefficients(i, 2))
         else:
-            loop(7, lambda i: coefficients(jnp.minimum(i, 3), jnp.where(i < 3, 2, i - 3)))
-
-    def finish(i):
-        m, k = i // 4, i % 4
-        q_copy(m, k).wait_recv()
-        block = jnp.where(d == 0, (x + k) % 4, (y + k) % 4)
-        place = jnp.where(m < 2, jnp.where(m == 0, places[0], places[1]), jnp.where(m == 2, places[2], places[3]))
-        cols = pl.ds(pl.multiple_of(block * 128, 128), 128)
-        for h in range(2):
-            rows = pl.ds(pl.multiple_of(place * 128 + h * 64, 64), 64)
-            out_ref[rows, cols] = squares[k, m, h] + sq_recv[k, m, h].astype(F32)
+            loop(3, lambda i: coefficients(n + 1, i + i // 2))
+        for m, k in tiles[n]:
+            c = q_copy(m, k)
+            c.start()
+            pending.append(c)
+
+    def finish(n):
+        for m, k in tiles[n]:
+            q_copy(m, k).wait_recv()
+        for m, k in tiles[n]:
+            block = jnp.where(d == 0, (x + k) % 4, (y + k) % 4)
+            cols = pl.ds(pl.multiple_of(block * 128, 128), 128)
+            rows = pl.ds(pl.multiple_of(places[m] * 128, 128), 128)
+            out_ref[rows, cols] = squares[k, m] + sq_recv[k, m].astype(F32)
 
     def grads(rel):
         if rel == 2:
@@ -381,15 +370,22 @@
         "a": acts, "g": grads, "zb": z_pair(2), "zc": z_pair(3), "xd": x_dep, "xf": x_fin, "zf": z_fin, "yf": y_fin,
         "az": az, "gy": gy, "gx": gx_forward, "gf": gf_arrived, "m": mask, "t": batch,
     }
+    issued, done = {}, [0]
+
+    def drain(count):
+        while done[0] < count:
+            pending[done[0]].wait_send()
+            done[0] += 1
+
     for name, *where in SCHEDULE:
-        steps[name](*where)
-    loop(16, finish)
-    for c in pending:
-        if isinstance(c, tuple):
-            loop(c[0], lambda t, make=c[1]: make(t).wait_send())
+        if name == "d":
+            drain(issued[tuple(where)])
         else:
-            c.wait_send()
-    loop(16, lambda i: q_copy(i // 4, i % 4).wait_send())
+            steps[name](*where)
+            issued[(name, *where)] = len(pending)
+    for n in range(4):
+        finish(n)
+    drain(len(pending))
 
 
 def local(activations, grad_outputs, act_basis, grad_basis, seq_lengths, old_eigen):
@@ -417,11 +413,11 @@
             vm((2, 4, 4, 128, 128), BF16),
             vm((2, 4, 4, 128, 128), BF16),
             vm((8, 4, 128, 128), BF16),
-            vm((4, 2, 4, 64, 1024), BF16),
-            vm((4, 4, 2, 64, 128), F32),
-            vm((4, 4, 2, 64, 128), BF16),
-            vm((4, 4, 2, 64, 128), BF16),
-            dma((5,)),
+            vm((4, 4, 128, 1024), BF16),
+            vm((4, 4, 128, 128), F32),
+            vm((4, 4, 128, 128), BF16),
+            vm((4, 4, 128, 128), BF16),
+            dma((14,)),
             dma((2, 2, 4)), dma((2, 2, 4)),
             dma((2, 2, 4, 2)), dma((2, 2, 4, 2)),
             dma((2, 4, 4)), dma((2, 4, 4)),

time: 53.8 us -> 52.6 us (0.978)
  Pallas kernels: 52.5 us -> 51.3 us
    pallas_call x1, Pallas kernels: 52.5 us -> 51.3 us  [local(): pl.pallas_call(kernel, out_shape=pltpu.VMEM((512, 512), F32), in_specs=[a...]
where the time goes in v2:
time: 52.6 us
  Pallas kernels  51.3 us (98%)
  other arithmetic  1.22 us (2%)
    pallas_call x1, Pallas kernels, local(): pl.pallas_call(kernel, out_shape=pltpu.VMEM((512, 512), F32), in_specs=[a...  51.3 us
    add x1, other arithmetic, local(): return 0.9 * old_eigen + 0.1 / 2048.0 * squares  1.22 us

profile of v2, /device:TPU:1, one launch (start us, length us, event | category | flops | bytes accessed | tf_op | source)
XLA Modules:
  0.0 52.6 jit_solution(2342245436207332830)
XLA Ops:
  0.0 0.0 copy-start
  0.0 51.3 %rotate_and_square.1 = f32[512,512]{1,0:T(8,128)S(1)} custom-call(bf16[1024,1024]{1,0:T(8,128)(2,1)} %act_hbm.1, bf16[1024,512]{1,0:T(8,128)(2,1)} %gout_hbm.1, bf16[1024,512]{1,0:T(8,128)(2,1)} %abasis_hbm.1, bf16[512,1024]{1,0:T(8,128)(2,1)} %gbasis_hbm.1, s32[1,4]{1,0:T(1,128)} %lengths_hbm.1), custom_call_target="tpu_custom_call" | custom-call | tf_op jit(solution)/shard_map/rotate_and_square/pallas_call | solution.py:395
  51.3 0.0 copy-done
  51.3 1.2 %multiply_add_fusion = f32[512,512]{1,0:T(8,128)} fusion(f32[512,512]{1,0:T(8,128)S(1)} %rotate_and_square.1, f32[512,512]{1,0:T(8,128)S(1)} %copy-done), kind=kLoop, calls=%fused_computation | loop fusion | flops 786432 | bytes 3145728 | tf_op jit(solution)/shard_map/add | solution.py:437
Async XLA Ops:
  0.0 51.3 %copy-start = (f32[512,512]{1,0:T(8,128)S(1)}, f32[512,512]{1,0:T(8,128)}, u32[]{:S(2)}) copy-start(f32[512,512]{1,0:T(8,128)} %param.11) | copy-start | bytes 3145732
